TPU v7x, 256 devices: a whole 4x4x8 slice. The times are simulated.
256 devices in a mesh: seq: 8 (over y, z_lo), head: 32 (over x, z_hi, core).
Axes of the slice: x: 4, y: 4, z: 8 (z_hi: 4, z_lo: 2; z = z_hi * 2 + z_lo), core: 2. Of those that a mesh axis runs over, the one named last changes fastest.
Arguments:
- queries: bfloat16 [2048, 128, 576], P('seq', 'head'), may hold values from -200 to 200
- latent_cache: bfloat16 [2048, 576], P('seq'), may hold values from -6 to 6
- grad_output: bfloat16 [2048, 128, 512], P('seq', 'head'), may hold values from -6 to 6
- query_blocks: int32 [8], replicated, may hold values from 0 to 127, as said below
- key_blocks: int32 [8], replicated, may hold values from 0 to 127, as said below
Outputs:
- grad_queries: bfloat16 [2048, 128, 576], P('seq', 'head')
- grad_cache: float32 [2048, 576], P(('seq', 'head'))
Inputs may be any that keep to these rules, and one draw needn't show every extreme that they name: `query_blocks`: the groups hold distinct block positions, one of them 16 * 8 - 1. `key_blocks`: the groups hold distinct block positions, one of them 0 and one 16 * 8 - 1.
All inputs are finite; a program needn't handle non-finite values.
Results may differ from a plain program's by a relative error of at most 0.013.
Values may be sent and summed in bfloat16 or wider, within the bound.
No kernel may reach another device: no remote copies, remote signals or barrier semaphores. Data moves between devices by JAX's collectives and lax.ppermute only.
A program may use at most 64 MiB of HBM per device.

v0:
```python
import jax
import jax.numpy as jnp
from jax import lax
from jax.sharding import PartitionSpec as P

DL = 512
DR = 64
softmax_scale = 0.07216878364870322


def shards(queries, latent_cache, grad_output, query_blocks, key_blocks):
    gathered = lax.all_gather(latent_cache, "seq", axis=0, tiled=True)
    tile_rows = queries.shape[0]
    group_index = lax.axis_index("seq")
    offsets = jnp.arange(tile_rows, dtype=jnp.int32)
    query_pos = query_blocks[group_index] * tile_rows + offsets
    key_pos = (key_blocks[:, None] * tile_rows + offsets[None, :]).reshape(-1)
    values = gathered[:, :DL]
    scores = softmax_scale * jnp.einsum(
        "qhd,kd->qhk", queries, gathered, preferred_element_type=jnp.float32
    )
    visible = key_pos[None, None, :] <= query_pos[:, None, None]
    masked = jnp.where(visible, scores, -jnp.inf)
    row_max = jnp.max(masked, axis=-1, keepdims=True)
    weights = jnp.exp(masked - row_max)
    probability = weights / jnp.sum(weights, axis=-1, keepdims=True)
    prob_bf16 = probability.astype(jnp.bfloat16)
    grad_probs = jnp.einsum("qhe,ke->qhk", grad_output, values, preferred_element_type=jnp.float32)
    output = jnp.einsum("qhk,ke->qhe", prob_bf16, values, preferred_element_type=jnp.float32)
    correction = jnp.sum(grad_output.astype(jnp.float32) * output, axis=-1, keepdims=True)
    grad_scores = (softmax_scale * probability * (grad_probs - correction)).astype(jnp.bfloat16)
    grad_queries = jnp.einsum(
        "qhk,kd->qhd", grad_scores, gathered, preferred_element_type=jnp.float32
    ).astype(jnp.bfloat16)
    grad_keys = jnp.einsum("qhk,qhd->kd", grad_scores, queries, preferred_element_type=jnp.float32)
    grad_values = jnp.einsum(
        "qhk,qhe->ke", prob_bf16, grad_output, preferred_element_type=jnp.float32
    )
    zeros_rope = jnp.zeros((grad_values.shape[0], DR), jnp.float32)
    partial_value = grad_keys + jnp.concatenate([grad_values, zeros_rope], axis=1)
    grad_cache = lax.psum_scatter(partial_value, ("seq", "head"), scatter_dimension=0, tiled=True)
    return (grad_queries, grad_cache)


def solution(mesh):
    placed = (P("seq", "head", None), P("seq", None), P("seq", "head", None), P(), P())
    return jax.shard_map(
        shards,
        mesh=mesh,
        in_specs=placed,
        out_specs=(P("seq", "head", None), P(("seq", "head"), None)),
        check_vma=False,
    )
```

profile of v0, /device:TPU:2, one launch (start us, length us, event | category | flops | bytes accessed | tf_op | source)
XLA Modules:
  0.0 385.2 jit_solution(10992031810698439277)
XLA Ops:
  7.2 0.0 copy-start
  7.2 0.0 all-gather.2.cloned.1.call-start
  7.2 0.7 all-gather.2.cloned.1.call-update
  7.9 0.0 all-reduce.4.cloned.1.call-start
  8.0 0.7 broadcast_multiply_fusion
  8.6 0.1 add_bitcast_fusion
  8.7 1.2 dynamic_slice.3
  10.6 0.4 broadcast_compare_fusion
  11.0 59.7 %all-gather.2.cloned.1.call-done = bf16[2048,576]{0,1:T(8,128)(2,1)} async-done(((bf16[256,576]{0,1:T(8,128)(2,1)}), bf16[2048,576]{0,1:T(8,128)(2,1)}) %all-gather.2.cloned.1.call-update) | async-done | bytes 2359312 | tf_op jit(solution)/shard_map/all_gather | solution.py:12
  70.7 0.0 copy-done
  70.7 7.3 %fusion.8 = f32[256,4,2048]{2,0,1:T(8,128)} fusion(bf16[256,4,576]{0,2,1:T(8,128)(2,1)S(1)} %copy-done, bf16[2048,576]{0,1:T(8,128)(2,1)} %all-gather.2.cloned.1.call-done), kind=kOutput, calls=%fused_computation.14 | convolution fusion | flops 2415919104 | bytes 11927552 | tf_op jit(solution)/shard_map/qhd,kd->qhk/dot_general | solution.py:19
  78.0 9.4 %fusion.17 = (f32[256,4]{0,1:T(4,128)S(1)}, f32[256,4,2048]{2,0,1:T(8,128)S(1)}) fusion(f32[256,4,2048]{2,0,1:T(8,128)} %fusion.8, pred[256,2048]{1,0:T(8,128)(4,1)S(1)} %broadcast_compare_fusion), kind=kOutput, calls=%fused_computation.28 | output fusion | flops 12584959 | bytes 17305600 | tf_op jit(solution)/shard_map/sub | solution.py:25
  87.4 0.0 copy-start.2
  87.4 1.4 fusion.5
  88.8 0.0 copy-done.2
  88.8 0.0 copy-start.1
  88.8 2.5 convolution_bitcast_fusion
  91.3 0.0 copy-done.1
  91.3 2.5 multiply_reduce_fusion
  93.8 3.3 multiply_convert_fusion
  97.1 0.0 copy-start.3
  97.1 2.1 copy-done.3
  99.2 5.3 %bitcast_add_fusion = f32[2048,576]{1,0:T(8,128)} fusion(f32[2048,512]{1,0:T(8,128)S(1)} %convolution_bitcast_fusion, bf16[256,4,2048]{2,0,1:T(8,128)(2,1)S(1)} %multiply_convert_fusion, bf16[256,4,576]{0,2,1:T(8,128)(2,1)S(1)} %copy-done), kind=kOutput, calls=%fused_computation.5 | convolution fusion | flops 2417098752 | bytes 14286848 | tf_op jit(solution)/shard_map/qhk,qhd->kd/dot_general | solution.py:35
  104.5 0.0 all-reduce.4.cloned.1.call-update
  104.5 5.8 %fusion.10 = bf16[256,4,576]{0,2,1:T(8,128)(2,1)} fusion(bf16[256,4,2048]{2,0,1:T(8,128)(2,1)} %copy-done.3, bf16[2048,576]{0,1:T(8,128)(2,1)S(1)} %copy-done.1), kind=kOutput, calls=%fused_computation.18 | convolution fusion | flops 2416508928 | bytes 7733248 | tf_op jit(solution)/shard_map/qhk,kd->qhd/dot_general | solution.py:32
  110.4 266.7 %all-reduce.4.cloned.1.call-done = f32[2048,576]{1,0:T(8,128)} async-done(((f32[2048,576]{1,0:T(8,128)}), f32[2048,576]{1,0:T(8,128)}) %all-reduce.4.cloned.1.call-update) | async-done | bytes 4718608
  377.0 1.3 constant_dynamic-slice_fusion
  (2 shorter events, 0.0 us)
Async XLA Ops:
  7.2 63.5 %copy-start = (bf16[256,4,576]{0,2,1:T(8,128)(2,1)S(1)}, bf16[256,4,576]{0,2,1:T(8,128)(2,1)}, u32[]{:S(2)}) copy-start(bf16[256,4,576]{0,2,1:T(8,128)(2,1)} %param.5) | copy-start | bytes 3538948
  7.2 63.5 %all-gather.2.cloned.1.call-start = ((), (), s32[]{:S(2)}) async-start(), calls=%async_computation | async-start | bytes 2654208 | tf_op jit(solution)/shard_map/all_gather | solution.py:12
  7.9 369.1 %all-reduce.4.cloned.1.call-start = ((), (), s32[]{:S(2)}) async-start(), calls=%async_computation.1 | async-start | bytes 10485760
  87.4 1.4 copy-start.2
  88.8 2.5 copy-start.1
  97.1 2.1 copy-start.3
Sparse Core Ops, SparseCore 0:
  9.7 60.8 all-gather.1
  104.6 272.3 all-reduce.3
where the time goes:
time: 385 us
  waiting for transfers between devices  327 us (85%)
  matrix products  26.7 us (7%)
  between operations  14.8 us (4%)
  other arithmetic  11.9 us (3%)
  local copies, waits for them, and re-layouts  4.67 us (1%)
    unnamed x3, waiting for transfers between devices  267 us
    all_gather x1, waiting for transfers between devices, shards(): gathered = lax.all_gather(latent_cache, 'seq', axis=0, tiled=True)  59.7 us
    sub x1, other arithmetic, shards(): weights = jnp.exp(masked - row_max)  9.45 us
  transfers between devices with their start and end apart: 2, of which 2 were waited for; matrix products, arithmetic and copies ran while one was open for 2% of the time, Pallas kernels for 0%

commit v1 on v0

--- a/solution.py
+++ b/solution.py
@@ -9,7 +9,10 @@
 
 
 def shards(queries, latent_cache, grad_output, query_blocks, key_blocks):
-    gathered = lax.all_gather(latent_cache, "seq", axis=0, tiled=True)
+    size = lax.axis_size("seq")
+    shards_2 = jnp.stack([latent_cache for _ in range(size)])
+    shards_2 = lax.all_to_all(shards_2, "seq", split_axis=0, concat_axis=0)
+    gathered = jnp.concatenate(shards_2, axis=0)
     tile_rows = queries.shape[0]
     group_index = lax.axis_index("seq")
     offsets = jnp.arange(tile_rows, dtype=jnp.int32)

time: 385 us -> 367 us (0.953)
  waiting for transfers between devices: 327 us -> 292 us
  local copies, waits for them, and re-layouts: 4.67 us -> 17.8 us
  other arithmetic: 11.9 us -> 5.94 us
  starting transfers between devices: 0.08 us -> 5.86 us
    all_gather x1 -> x0, waiting for transfers between devices: 59.7 us -> none  [shards(): gathered = lax.all_gather(latent_cache, 'seq', axis=0, tiled=True)]
    all_to_all x0 -> x1, waiting for transfers between devices: none -> 27.2 us  [shards(): shards_2 = lax.all_to_all(shards_2, 'seq', split_axis=0, concat_axis=0)]
    sub x0 -> x1, matrix products: none -> 10.2 us  [shards(): weights = jnp.exp(masked - row_max)]
    sub x1 -> x0, other arithmetic: 9.45 us -> none  [shards(): weights = jnp.exp(masked - row_max)]
    dot_general x1 -> x0, matrix products: 7.3 us -> none  [shards(): jnp.einsum('qhd,kd->qhk', queries, gathered, preferred_element_type=jnp.f...]
    reshape x0 -> x2, local copies, waits for them, and re-layouts: none -> 6.77 us  [shards(): gathered = jnp.concatenate(shards_2, axis=0)]
    all_to_all x0 -> x1, starting transfers between devices: none -> 5.82 us  [shards(): shards_2 = lax.all_to_all(shards_2, 'seq', split_axis=0, concat_axis=0)]
    unnamed x3 -> x2, waiting for transfers between devices: 267 us -> 265 us
where the time goes in v1:
time: 367 us; the launch traced here: 366 us
  waiting for transfers between devices  292 us (80%)
  matrix products  29.6 us (8%)
  local copies, waits for them, and re-layouts  17.8 us (5%)
  between operations  14.8 us (4%)
  other arithmetic  5.94 us (2%)
  starting transfers between devices  5.86 us (2%)
    unnamed x2, waiting for transfers between devices  265 us
    all_to_all x1, waiting for transfers between devices, shards(): shards_2 = lax.all_to_all(shards_2, 'seq', split_axis=0, concat_axis=0)  27.2 us
    sub x1, matrix products, shards(): weights = jnp.exp(masked - row_max)  10.2 us
  transfers between devices with their start and end apart: 2, of which 2 were waited for; matrix products, arithmetic and copies ran while one was open for 2% of the time, Pallas kernels for 0%

profile of v1, /device:TPU:2, one launch (start us, length us, event | category | flops | bytes accessed | tf_op | source)
XLA Modules:
  0.0 366.1 jit_solution(1121639650477886250)
XLA Ops:
  7.2 0.0 copy-start
  7.2 0.0 copy-start.4
  7.2 0.0 copy-start.5
  7.2 2.6 stack.2
  9.8 5.8 %all-to-all-start = ((bf16[8,256,576]{1,2,0:T(8,128)(2,1)}), bf16[8,256,576]{1,2,0:T(8,128)(2,1)S(1)}, u32[]{:S(2)}, u32[]{:S(2)}) async-start(bf16[8,256,576]{1,2,0:T(8,128)(2,1)} %stack.2), calls=%async_computation | async-start | bytes 4718592 | tf_op jit(solution)/shard_map/all_to_all | solution.py:14
  15.6 0.0 all-reduce.4.cloned.1.call-start
  15.7 0.0 copy-done.4
  15.7 0.1 add_bitcast_fusion
  15.8 0.0 copy-done.5
  15.8 0.6 dynamic_slice.3
  17.0 1.2 broadcast_compare_fusion
  18.2 27.2 %all-to-all-done = bf16[8,256,576]{1,2,0:T(8,128)(2,1)S(1)} async-done(((bf16[8,256,576]{1,2,0:T(8,128)(2,1)}), bf16[8,256,576]{1,2,0:T(8,128)(2,1)S(1)}, u32[]{:S(2)}, u32[]{:S(2)}) %all-to-all-start) | async-done | bytes 2359328 | tf_op jit(solution)/shard_map/all_to_all | solution.py:14
  45.4 2.7 copy.14
  48.2 5.0 %reshape.65 = bf16[2048,576,1]{0,1,2:T(8,128)(2,1)} reshape(bf16[8,256,576]{1,0,2:T(8,128)(2,1)} %copy.14) | data formatting | bytes 4718592 | tf_op jit(solution)/shard_map/reshape | solution.py:15
  53.2 1.8 copy.29
  54.9 0.0 copy-done
  54.9 10.2 %fusion.10 = (f32[256,4]{0,1:T(4,128)S(1)}, f32[256,4,2048]{2,0,1:T(8,128)}) fusion(pred[256,2048]{1,0:T(8,128)(4,1)} %broadcast_compare_fusion, bf16[256,4,576]{0,2,1:T(8,128)(2,1)S(1)} %copy-done, bf16[2048,576,1]{0,1,2:T(8,128)(2,1)} %reshape.65), kind=kOutput, calls=%fused_computation.24 | convolution fusion | flops 2424309760 | bytes 12455936 | tf_op jit(solution)/shard_map/sub | solution.py:28
  65.1 4.7 %fusion.5 = bf16[256,4,2048]{2,0,1:T(8,128)(2,1)S(1)} fusion(f32[256,4,2048]{2,0,1:T(8,128)} %get-tuple-element.3, f32[256,4]{0,1:T(4,128)S(1)} %get-tuple-element.2), kind=kLoop, calls=%fused_computation.10 | loop fusion | flops 4194304 | bytes 12587008 | tf_op jit(solution)/shard_map/convert_element_type | solution.py:30
  69.8 0.0 copy-done.3
  69.9 0.0 slice-start
  69.9 2.4 convolution_bitcast_fusion
  72.3 0.0 slice-start.1
  72.3 2.5 multiply_reduce_fusion
  74.8 3.4 multiply_convert_fusion
  78.2 0.0 copy-start.6
  78.2 2.1 copy-done.6
  80.3 5.3 %bitcast_add_fusion = f32[2048,576]{1,0:T(8,128)} fusion(f32[2048,512]{1,0:T(8,128)S(1)} %convolution_bitcast_fusion, bf16[256,4,2048]{2,0,1:T(8,128)(2,1)S(1)} %multiply_convert_fusion, bf16[256,4,576]{0,2,1:T(8,128)(2,1)S(1)} %copy-done), kind=kOutput, calls=%fused_computation.5 | convolution fusion | flops 2417098752 | bytes 14286848 | tf_op jit(solution)/shard_map/qhk,qhd->kd/dot_general | solution.py:38
  85.5 0.0 all-reduce.4.cloned.1.call-update
  85.6 1.6 copy-done.1
  87.2 5.8 %convolution_convert_fusion = bf16[256,4,576]{0,2,1:T(8,128)(2,1)} fusion(bf16[256,4,2048]{2,0,1:T(8,128)(2,1)} %copy-done.6, bf16[2048,576,1]{0,1,2:T(8,128)(2,1)S(1)} %copy-done.1), kind=kOutput, calls=%fused_computation.14 | convolution fusion | flops 2416508928 | bytes 7733248 | tf_op jit(solution)/shard_map/qhk,kd->qhd/dot_general | solution.py:35
  93.0 264.9 %all-reduce.4.cloned.1.call-done = f32[2048,576]{1,0:T(8,128)} async-done(((f32[2048,576]{1,0:T(8,128)}), f32[2048,576]{1,0:T(8,128)}) %all-reduce.4.cloned.1.call-update) | async-done | bytes 4718608
  357.9 1.3 constant_dynamic-slice_fusion
  (10 shorter events, 0.0 us)
Async XLA Ops:
  7.2 47.8 %copy-start = (bf16[256,4,576]{0,2,1:T(8,128)(2,1)S(1)}, bf16[256,4,576]{0,2,1:T(8,128)(2,1)}, u32[]{:S(2)}) copy-start(bf16[256,4,576]{0,2,1:T(8,128)(2,1)} %param.5) | copy-start | bytes 3538948
  7.2 8.5 %copy-start.4 = (s32[8]{0:T(128)S(1)}, s32[8]{0:T(128)}, u32[]{:S(2)}) copy-start(s32[8]{0:T(128)} %param.9) | copy-start | bytes 100
  7.2 8.6 %copy-start.5 = (s32[8]{0:T(128)S(1)}, s32[8]{0:T(128)}, u32[]{:S(2)}) copy-start(s32[8]{0:T(128)} %param.8) | copy-start | bytes 100
  9.8 35.6 %all-to-all-start = ((bf16[8,256,576]{1,2,0:T(8,128)(2,1)}), bf16[8,256,576]{1,2,0:T(8,128)(2,1)S(1)}, u32[]{:S(2)}, u32[]{:S(2)}) async-start(bf16[8,256,576]{1,2,0:T(8,128)(2,1)} %stack.2), calls=%async_computation | async-start | bytes 4718592 | tf_op jit(solution)/shard_map/all_to_all | solution.py:14
  15.6 342.3 %all-reduce.4.cloned.1.call-start = ((), (), s32[]{:S(2)}) async-start(), calls=%async_computation.1 | async-start | bytes 10485760
  65.1 4.7 %copy-start.3 = (bf16[256,4,512]{2,1,0:T(4,128)(2,1)S(1)}, bf16[256,4,512]{2,1,0:T(4,128)(2,1)}, u32[]{:S(2)}) copy-start(bf16[256,4,512]{2,1,0:T(4,128)(2,1)} %param.7) | copy-start | bytes 3145732
  69.8 2.4 copy-start.2
  69.9 5.0 %slice-start = ((s8[8388608]{0:T(1024)(128)(4,1)}), s8[4194304]{0:T(1024)(128)(4,1)S(1)}, s32[]{:S(2)}) async-start(s8[8388608]{0:T(1024)(128)(4,1)} %bitcast.28), calls=%async_computation.2 | async-start | bytes 8388608
  72.3 2.5 slice-start.1
  78.2 2.1 copy-start.6
  85.5 1.7 copy-start.1
Sparse Core Ops, SparseCore 0:
  85.7 272.1 all-reduce.3
